TPU v7x, 256 devices: a whole 4x4x8 slice. The times are simulated.
256 devices in a mesh: grp: 16 (over y_lo, z), blk: 16 (over x, y_hi, core).
Axes of the slice: x: 4, y: 4 (y_hi: 2, y_lo: 2; y = y_hi * 2 + y_lo), z: 8, core: 2. Of those that a mesh axis runs over, the one named last changes fastest.
Arguments:
- encoded_anchor: bfloat16 [131072, 256], P(('grp', 'blk')), parts along dimension 0, may hold values from -1 to 1
- encoded_target: bfloat16 [131072, 256], P(('grp', 'blk')), parts along dimension 0, may hold values from -1 to 1
- matched_target: int32 [131072], P(('grp', 'blk')), parts along dimension 0, may hold values from 0 to 8191, as said below
- anchor_logzeta: float32 [131072], P(('grp', 'blk')), parts along dimension 0, may hold values from 0 to 20, as said below
- target_logzeta_saved: float32 [131072], P(('grp', 'blk')), parts along dimension 0, may hold values from 0 to 20, as said below
- heat_values: float32 [64], P('grp'), parts along dimension 0, may hold values from 0 to 1
- matchup_position: int32 [16], P('grp'), parts along dimension 0, may hold values from 0 to 3
Outputs:
- gradient_view_a: float32 [131072, 256], P(('grp', 'blk')), parts along dimension 0
- gradient_view_b: float32 [131072, 256], P(('grp', 'blk')), parts along dimension 0
There are 16 independent parts, one for each index of `grp`. A program takes and returns all parts, laid end to end along the dimension named above; each array names one. Nothing has to cross between parts.
Inputs may be any that keep to these rules, and one draw needn't show every extreme that they name: `matched_target`: each view-B node is the partner of exactly one view-A node. anchor_logzeta[i] is the log of the sum over j of exp(scores[i, j]), computed from the same unit vectors and temperature. target_logzeta_saved[j] is the log of the sum over i of exp(scores[i, j]).
All inputs are finite; a program needn't handle non-finite values.
Results may differ from a plain program's by a relative error of at most 0.0041.
Values may be sent and summed in bfloat16 or wider, within the bound.
A program may use at most 64 MiB of HBM per device.

v0:
```python
import jax
import jax.numpy as jnp
from jax import lax
from jax.sharding import PartitionSpec as P


def passed_along(value, axis, steps):
    count = lax.axis_size(axis)
    pairs = [(source, (source + steps) % count) for source in range(count)]
    return lax.ppermute(value, axis, pairs)


def normalize(embed):
    floats = embed.astype(jnp.float32)
    inverse = lax.rsqrt(jnp.sum(floats * floats, axis=1, keepdims=True) + 1e-06)
    unit_float = floats * inverse
    return (inverse, unit_float.astype(jnp.bfloat16), unit_float)


def probability_linkage(
    sphere_anchors,
    sphere_targets,
    anchor_logzeta_local,
    target_logzeta,
    matched_entries,
    target_extent,
    heat_scale,
):
    cosine_logits = (
        lax.dot_general(
            sphere_anchors,
            sphere_targets,
            (((1,), (1,)), ((), ())),
            preferred_element_type=jnp.float32,
        )
        / heat_scale
    )
    paired = (matched_entries[:, None] == target_extent[None, :]).astype(jnp.float32)
    probability_share = (
        jnp.exp(cosine_logits - anchor_logzeta_local[:, None])
        + jnp.exp(cosine_logits - target_logzeta[None, :])
        - 2.0 * paired
    )
    return probability_share.astype(jnp.bfloat16)


def finalize_gradient(dunit, inverse, unit_float):
    return inverse * (dunit - unit_float * jnp.sum(unit_float * dunit, axis=1, keepdims=True))


def on_device(
    encoded_anchor,
    encoded_target,
    matched_target,
    anchor_logzeta,
    target_logzeta_saved,
    heat_values,
    matchup_position,
):
    rows_here = encoded_anchor.shape[0]
    width = encoded_anchor.shape[1]
    cycle_size = lax.axis_size("blk")
    position = lax.axis_index("blk")
    heat_scale = jnp.sum(
        jnp.where(
            jnp.arange(heat_values.shape[0], dtype=jnp.int32) == matchup_position[0],
            heat_values,
            jnp.zeros_like(heat_values),
        )
    )
    reciprocal_length_anchor, scaled_anchor_vectors, float_anchor_vectors = normalize(
        encoded_anchor
    )
    reciprocal_length_target, scaled_target_vectors, float_target_vectors = normalize(
        encoded_target
    )
    block_offsets = jnp.arange(rows_here, dtype=jnp.int32)
    logz_all = lax.all_gather(target_logzeta_saved, "blk", axis=0, tiled=True)

    def tile(sphere_targets, source):
        first_block = source * rows_here
        target_logzeta = lax.dynamic_slice_in_dim(logz_all, first_block, rows_here, 0)
        probability_share = probability_linkage(
            scaled_anchor_vectors,
            sphere_targets,
            anchor_logzeta,
            target_logzeta,
            matched_target,
            first_block + block_offsets,
            heat_scale,
        )
        sphere_derivative_entries = jnp.dot(
            probability_share, sphere_targets, preferred_element_type=jnp.float32
        )
        col_terms = lax.dot_general(
            probability_share,
            scaled_anchor_vectors,
            (((0,), (0,)), ((), ())),
            preferred_element_type=jnp.float32,
        )
        return (sphere_derivative_entries, col_terms)

    zeros_rows = jnp.zeros((rows_here, width), jnp.float32)

    def visit(state, visit_index):
        moving, col_sums, sphere_derivative_entries = state
        source = (position - visit_index) % cycle_size
        more_rows, col_terms = tile(moving, source)
        moving = passed_along(moving, "blk", 1)
        col_sums = passed_along(col_sums + col_terms, "blk", 1)
        return ((moving, col_sums, sphere_derivative_entries + more_rows), None)

    final_state, unused = lax.scan(
        visit,
        (scaled_target_vectors, zeros_rows, zeros_rows),
        jnp.arange(cycle_size, dtype=jnp.int32),
    )
    target_derivative = final_state[1]
    sphere_derivative_anchor = final_state[2]
    gradient_view_a = finalize_gradient(
        sphere_derivative_anchor / heat_scale, reciprocal_length_anchor, float_anchor_vectors
    )
    gradient_view_b = finalize_gradient(
        target_derivative / heat_scale, reciprocal_length_target, float_target_vectors
    )
    return (gradient_view_a, gradient_view_b)


def solution(mesh):
    return jax.shard_map(
        on_device,
        mesh=mesh,
        in_specs=(
            P(("grp", "blk"), None),
            P(("grp", "blk"), None),
            P(("grp", "blk")),
            P(("grp", "blk")),
            P(("grp", "blk")),
            P("grp"),
            P("grp"),
        ),
        out_specs=(P(("grp", "blk"), None), P(("grp", "blk"), None)),
        check_vma=False,
    )
```

profile of v0, /device:TPU:128, one launch (start us, length us, event | category | flops | bytes accessed | tf_op | source)
XLA Modules:
  0.0 325.0 jit_solution(10663134384561113737)
XLA Ops:
  1.3 1.3 fusion.16
  2.7 1.1 fusion.11
  4.0 0.7 copy-done.2
  4.6 24.4 %all-gather = f32[16,1,512]{2,1,0:T(1,128)S(1)} all-gather(f32[1,1,512]{2,1,0:T(1,128)S(1)} %bitcast.26), channel_id=1, replica_groups=mesh['grp'=16,'blk'=16] {'blk'}, dimensions={0}, use_global_device_ids=true | all-gather | bytes 34816 | tf_op jit(solution)/shard_map/all_gather | solution.py:78
  29.1 0.8 copy-done.1
  30.2 0.6 copy-done.3
  30.8 289.6 %while.17 = (s32[]{:T(128)}, bf16[512,256]{1,0:T(8,128)(2,1)S(1)}, f32[512,256]{1,0:T(8,128)S(1)}, f32[512,256]{1,0:T(8,128)S(1)}, bf16[512,256]{1,0:T(8,128)(2,...) while((s32[]{:T(128)}, bf16[512,256]{1,0:T(8,128)(2,1)S(1)}, ...), condition=%wide.region_4.5_spmd.clone, body=%wide.region_3.4_spmd.clone.sunk | while | flops 405144064 | bytes 8403382 | solution.py:113
  30.8 0.6 dynamic_slice.17
  32.2 1.3 subtract_convert_fusion.2
  33.8 0.4 collective-permute-start.1
  34.7 14.2 %collective-permute-done = bf16[512,256]{1,0:T(8,128)(2,1)S(1)} collective-permute-done((bf16[512,256]{1,0:T(8,128)(2,1)S(1)}, bf16[512,256]{1,0:T(8,128)(2,1)S(1)}, u32[]{:S(2)}, u32[]{:S(2)}) %collective-permute-start) | collective-permute-done | bytes 262176 | tf_op jit(solution)/shard_map/while/body/eval_jaxpr/ppermute | solution.py:10
  48.9 0.6 dynamic_slice.17
  50.3 1.3 subtract_convert_fusion.2
  52.5 14.5 %collective-permute-done = bf16[512,256]{1,0:T(8,128)(2,1)S(1)} collective-permute-done((bf16[512,256]{1,0:T(8,128)(2,1)S(1)}, bf16[512,256]{1,0:T(8,128)(2,1)S(1)}, u32[]{:S(2)}, u32[]{:S(2)}) %collective-permute-start) | collective-permute-done | bytes 262176 | tf_op jit(solution)/shard_map/while/body/eval_jaxpr/ppermute | solution.py:10
  67.0 0.6 dynamic_slice.17
  68.4 1.3 subtract_convert_fusion.2
  70.2 0.4 convolution_add_fusion.5
  70.6 14.5 %collective-permute-done = bf16[512,256]{1,0:T(8,128)(2,1)S(1)} collective-permute-done((bf16[512,256]{1,0:T(8,128)(2,1)S(1)}, bf16[512,256]{1,0:T(8,128)(2,1)S(1)}, u32[]{:S(2)}, u32[]{:S(2)}) %collective-permute-start) | collective-permute-done | bytes 262176 | tf_op jit(solution)/shard_map/while/body/eval_jaxpr/ppermute | solution.py:10
  85.1 0.6 dynamic_slice.17
  86.5 1.3 subtract_convert_fusion.2
  88.3 0.4 convolution_add_fusion.5
  88.7 14.5 %collective-permute-done = bf16[512,256]{1,0:T(8,128)(2,1)S(1)} collective-permute-done((bf16[512,256]{1,0:T(8,128)(2,1)S(1)}, bf16[512,256]{1,0:T(8,128)(2,1)S(1)}, u32[]{:S(2)}, u32[]{:S(2)}) %collective-permute-start) | collective-permute-done | bytes 262176 | tf_op jit(solution)/shard_map/while/body/eval_jaxpr/ppermute | solution.py:10
  103.2 0.6 dynamic_slice.17
  104.6 1.3 subtract_convert_fusion.2
  106.8 14.5 %collective-permute-done = bf16[512,256]{1,0:T(8,128)(2,1)S(1)} collective-permute-done((bf16[512,256]{1,0:T(8,128)(2,1)S(1)}, bf16[512,256]{1,0:T(8,128)(2,1)S(1)}, u32[]{:S(2)}, u32[]{:S(2)}) %collective-permute-start) | collective-permute-done | bytes 262176 | tf_op jit(solution)/shard_map/while/body/eval_jaxpr/ppermute | solution.py:10
  121.3 0.6 dynamic_slice.17
  122.7 1.3 subtract_convert_fusion.2
  124.9 14.5 %collective-permute-done = bf16[512,256]{1,0:T(8,128)(2,1)S(1)} collective-permute-done((bf16[512,256]{1,0:T(8,128)(2,1)S(1)}, bf16[512,256]{1,0:T(8,128)(2,1)S(1)}, u32[]{:S(2)}, u32[]{:S(2)}) %collective-permute-start) | collective-permute-done | bytes 262176 | tf_op jit(solution)/shard_map/while/body/eval_jaxpr/ppermute | solution.py:10
  139.4 0.6 dynamic_slice.17
  140.8 1.3 subtract_convert_fusion.2
  142.6 0.4 convolution_add_fusion.5
  143.0 14.5 %collective-permute-done = bf16[512,256]{1,0:T(8,128)(2,1)S(1)} collective-permute-done((bf16[512,256]{1,0:T(8,128)(2,1)S(1)}, bf16[512,256]{1,0:T(8,128)(2,1)S(1)}, u32[]{:S(2)}, u32[]{:S(2)}) %collective-permute-start) | collective-permute-done | bytes 262176 | tf_op jit(solution)/shard_map/while/body/eval_jaxpr/ppermute | solution.py:10
  157.5 0.6 dynamic_slice.17
  158.9 1.3 subtract_convert_fusion.2
  160.7 0.4 convolution_add_fusion.5
  161.1 14.5 %collective-permute-done = bf16[512,256]{1,0:T(8,128)(2,1)S(1)} collective-permute-done((bf16[512,256]{1,0:T(8,128)(2,1)S(1)}, bf16[512,256]{1,0:T(8,128)(2,1)S(1)}, u32[]{:S(2)}, u32[]{:S(2)}) %collective-permute-start) | collective-permute-done | bytes 262176 | tf_op jit(solution)/shard_map/while/body/eval_jaxpr/ppermute | solution.py:10
  175.6 0.6 dynamic_slice.17
  177.0 1.3 subtract_convert_fusion.2
  179.2 14.5 %collective-permute-done = bf16[512,256]{1,0:T(8,128)(2,1)S(1)} collective-permute-done((bf16[512,256]{1,0:T(8,128)(2,1)S(1)}, bf16[512,256]{1,0:T(8,128)(2,1)S(1)}, u32[]{:S(2)}, u32[]{:S(2)}) %collective-permute-start) | collective-permute-done | bytes 262176 | tf_op jit(solution)/shard_map/while/body/eval_jaxpr/ppermute | solution.py:10
  193.7 0.6 dynamic_slice.17
  195.1 1.3 subtract_convert_fusion.2
  197.3 14.5 %collective-permute-done = bf16[512,256]{1,0:T(8,128)(2,1)S(1)} collective-permute-done((bf16[512,256]{1,0:T(8,128)(2,1)S(1)}, bf16[512,256]{1,0:T(8,128)(2,1)S(1)}, u32[]{:S(2)}, u32[]{:S(2)}) %collective-permute-start) | collective-permute-done | bytes 262176 | tf_op jit(solution)/shard_map/while/body/eval_jaxpr/ppermute | solution.py:10
  211.8 0.6 dynamic_slice.17
  213.2 1.3 subtract_convert_fusion.2
  215.0 0.4 convolution_add_fusion.5
  215.4 14.5 %collective-permute-done = bf16[512,256]{1,0:T(8,128)(2,1)S(1)} collective-permute-done((bf16[512,256]{1,0:T(8,128)(2,1)S(1)}, bf16[512,256]{1,0:T(8,128)(2,1)S(1)}, u32[]{:S(2)}, u32[]{:S(2)}) %collective-permute-start) | collective-permute-done | bytes 262176 | tf_op jit(solution)/shard_map/while/body/eval_jaxpr/ppermute | solution.py:10
  229.9 0.6 dynamic_slice.17
  231.3 1.3 subtract_convert_fusion.2
  233.5 14.5 %collective-permute-done = bf16[512,256]{1,0:T(8,128)(2,1)S(1)} collective-permute-done((bf16[512,256]{1,0:T(8,128)(2,1)S(1)}, bf16[512,256]{1,0:T(8,128)(2,1)S(1)}, u32[]{:S(2)}, u32[]{:S(2)}) %collective-permute-start) | collective-permute-done | bytes 262176 | tf_op jit(solution)/shard_map/while/body/eval_jaxpr/ppermute | solution.py:10
  248.0 0.6 dynamic_slice.17
  249.4 1.3 subtract_convert_fusion.2
  251.6 14.5 %collective-permute-done = bf16[512,256]{1,0:T(8,128)(2,1)S(1)} collective-permute-done((bf16[512,256]{1,0:T(8,128)(2,1)S(1)}, bf16[512,256]{1,0:T(8,128)(2,1)S(1)}, u32[]{:S(2)}, u32[]{:S(2)}) %collective-permute-start) | collective-permute-done | bytes 262176 | tf_op jit(solution)/shard_map/while/body/eval_jaxpr/ppermute | solution.py:10
  266.1 0.6 dynamic_slice.17
  267.5 1.3 subtract_convert_fusion.2
  269.7 14.5 %collective-permute-done = bf16[512,256]{1,0:T(8,128)(2,1)S(1)} collective-permute-done((bf16[512,256]{1,0:T(8,128)(2,1)S(1)}, bf16[512,256]{1,0:T(8,128)(2,1)S(1)}, u32[]{:S(2)}, u32[]{:S(2)}) %collective-permute-start) | collective-permute-done | bytes 262176 | tf_op jit(solution)/shard_map/while/body/eval_jaxpr/ppermute | solution.py:10
  284.2 0.6 dynamic_slice.17
  285.6 1.3 subtract_convert_fusion.2
  287.8 14.5 %collective-permute-done = bf16[512,256]{1,0:T(8,128)(2,1)S(1)} collective-permute-done((bf16[512,256]{1,0:T(8,128)(2,1)S(1)}, bf16[512,256]{1,0:T(8,128)(2,1)S(1)}, u32[]{:S(2)}, u32[]{:S(2)}) %collective-permute-start) | collective-permute-done | bytes 262176 | tf_op jit(solution)/shard_map/while/body/eval_jaxpr/ppermute | solution.py:10
  302.3 0.6 dynamic_slice.17
  303.7 1.3 subtract_convert_fusion.2
  305.9 14.5 %collective-permute-done = bf16[512,256]{1,0:T(8,128)(2,1)S(1)} collective-permute-done((bf16[512,256]{1,0:T(8,128)(2,1)S(1)}, bf16[512,256]{1,0:T(8,128)(2,1)S(1)}, u32[]{:S(2)}, u32[]{:S(2)}) %collective-permute-start) | collective-permute-done | bytes 262176 | tf_op jit(solution)/shard_map/while/body/eval_jaxpr/ppermute | solution.py:10
  320.4 1.1 fusion.8
  321.6 1.7 fusion.14
  323.3 1.7 fusion.10
  (137 shorter events, 14.4 us)
Async XLA Ops:
  0.6 3.2 copy-start
  3.9 0.7 copy-start.2
  29.0 0.9 copy-start.1
  30.1 0.7 copy-start.3
  30.1 0.7 copy-start.4
  33.8 15.1 %collective-permute-start.1 = (f32[512,256]{1,0:T(8,128)S(1)}, f32[512,256]{1,0:T(8,128)S(1)}, u32[]{:S(2)}, u32[]{:S(2)}) collective-permute-start(f32[512,256]{1,0:T(8,128)S(1)} %convolution_add_fusion.4), channel_id=1, source_target_pairs={{0,1},{1,2},{2,3},{3,4},{4,5},{5,6},{6,7},{7,8},{8,9},{9,10},{10,1... | collective-permute-start | bytes 1572872 | tf_op jit(solution)/shard_map/while/body/eval_jaxpr/ppermute | solution.py:10
  34.2 14.7 %collective-permute-start = (bf16[512,256]{1,0:T(8,128)(2,1)S(1)}, bf16[512,256]{1,0:T(8,128)(2,1)S(1)}, u32[]{:S(2)}, u32[]{:S(2)}) collective-permute-start(bf16[512,256]{1,0:T(8,128)(2,1)S(1)} %copy.14), channel_id=1, source_target_pairs={{0,1},{1,2},{2,3},{3,4},{4,5},{5,6},{6,7},{7,8},{8,9},{9,10},{10,1... | collective-permute-start | bytes 786440 | tf_op jit(solution)/shard_map/while/body/eval_jaxpr/ppermute | solution.py:10
  51.9 15.1 %collective-permute-start.1 = (f32[512,256]{1,0:T(8,128)S(1)}, f32[512,256]{1,0:T(8,128)S(1)}, u32[]{:S(2)}, u32[]{:S(2)}) collective-permute-start(f32[512,256]{1,0:T(8,128)S(1)} %convolution_add_fusion.4), channel_id=1, source_target_pairs={{0,1},{1,2},{2,3},{3,4},{4,5},{5,6},{6,7},{7,8},{8,9},{9,10},{10,1... | collective-permute-start | bytes 1572872 | tf_op jit(solution)/shard_map/while/body/eval_jaxpr/ppermute | solution.py:10
  52.0 15.0 %collective-permute-start = (bf16[512,256]{1,0:T(8,128)(2,1)S(1)}, bf16[512,256]{1,0:T(8,128)(2,1)S(1)}, u32[]{:S(2)}, u32[]{:S(2)}) collective-permute-start(bf16[512,256]{1,0:T(8,128)(2,1)S(1)} %copy.14), channel_id=1, source_target_pairs={{0,1},{1,2},{2,3},{3,4},{4,5},{5,6},{6,7},{7,8},{8,9},{9,10},{10,1... | collective-permute-start | bytes 786440 | tf_op jit(solution)/shard_map/while/body/eval_jaxpr/ppermute | solution.py:10
  70.0 15.1 %collective-permute-start.1 = (f32[512,256]{1,0:T(8,128)S(1)}, f32[512,256]{1,0:T(8,128)S(1)}, u32[]{:S(2)}, u32[]{:S(2)}) collective-permute-start(f32[512,256]{1,0:T(8,128)S(1)} %convolution_add_fusion.4), channel_id=1, source_target_pairs={{0,1},{1,2},{2,3},{3,4},{4,5},{5,6},{6,7},{7,8},{8,9},{9,10},{10,1... | collective-permute-start | bytes 1572872 | tf_op jit(solution)/shard_map/while/body/eval_jaxpr/ppermute | solution.py:10
  70.1 15.0 %collective-permute-start = (bf16[512,256]{1,0:T(8,128)(2,1)S(1)}, bf16[512,256]{1,0:T(8,128)(2,1)S(1)}, u32[]{:S(2)}, u32[]{:S(2)}) collective-permute-start(bf16[512,256]{1,0:T(8,128)(2,1)S(1)} %copy.14), channel_id=1, source_target_pairs={{0,1},{1,2},{2,3},{3,4},{4,5},{5,6},{6,7},{7,8},{8,9},{9,10},{10,1... | collective-permute-start | bytes 786440 | tf_op jit(solution)/shard_map/while/body/eval_jaxpr/ppermute | solution.py:10
  88.1 15.1 %collective-permute-start.1 = (f32[512,256]{1,0:T(8,128)S(1)}, f32[512,256]{1,0:T(8,128)S(1)}, u32[]{:S(2)}, u32[]{:S(2)}) collective-permute-start(f32[512,256]{1,0:T(8,128)S(1)} %convolution_add_fusion.4), channel_id=1, source_target_pairs={{0,1},{1,2},{2,3},{3,4},{4,5},{5,6},{6,7},{7,8},{8,9},{9,10},{10,1... | collective-permute-start | bytes 1572872 | tf_op jit(solution)/shard_map/while/body/eval_jaxpr/ppermute | solution.py:10
  88.2 15.0 %collective-permute-start = (bf16[512,256]{1,0:T(8,128)(2,1)S(1)}, bf16[512,256]{1,0:T(8,128)(2,1)S(1)}, u32[]{:S(2)}, u32[]{:S(2)}) collective-permute-start(bf16[512,256]{1,0:T(8,128)(2,1)S(1)} %copy.14), channel_id=1, source_target_pairs={{0,1},{1,2},{2,3},{3,4},{4,5},{5,6},{6,7},{7,8},{8,9},{9,10},{10,1... | collective-permute-start | bytes 786440 | tf_op jit(solution)/shard_map/while/body/eval_jaxpr/ppermute | solution.py:10
  106.2 15.1 %collective-permute-start.1 = (f32[512,256]{1,0:T(8,128)S(1)}, f32[512,256]{1,0:T(8,128)S(1)}, u32[]{:S(2)}, u32[]{:S(2)}) collective-permute-start(f32[512,256]{1,0:T(8,128)S(1)} %convolution_add_fusion.4), channel_id=1, source_target_pairs={{0,1},{1,2},{2,3},{3,4},{4,5},{5,6},{6,7},{7,8},{8,9},{9,10},{10,1... | collective-permute-start | bytes 1572872 | tf_op jit(solution)/shard_map/while/body/eval_jaxpr/ppermute | solution.py:10
  106.3 15.0 %collective-permute-start = (bf16[512,256]{1,0:T(8,128)(2,1)S(1)}, bf16[512,256]{1,0:T(8,128)(2,1)S(1)}, u32[]{:S(2)}, u32[]{:S(2)}) collective-permute-start(bf16[512,256]{1,0:T(8,128)(2,1)S(1)} %copy.14), channel_id=1, source_target_pairs={{0,1},{1,2},{2,3},{3,4},{4,5},{5,6},{6,7},{7,8},{8,9},{9,10},{10,1... | collective-permute-start | bytes 786440 | tf_op jit(solution)/shard_map/while/body/eval_jaxpr/ppermute | solution.py:10
  124.3 15.1 %collective-permute-start.1 = (f32[512,256]{1,0:T(8,128)S(1)}, f32[512,256]{1,0:T(8,128)S(1)}, u32[]{:S(2)}, u32[]{:S(2)}) collective-permute-start(f32[512,256]{1,0:T(8,128)S(1)} %convolution_add_fusion.4), channel_id=1, source_target_pairs={{0,1},{1,2},{2,3},{3,4},{4,5},{5,6},{6,7},{7,8},{8,9},{9,10},{10,1... | collective-permute-start | bytes 1572872 | tf_op jit(solution)/shard_map/while/body/eval_jaxpr/ppermute | solution.py:10
  124.4 15.0 %collective-permute-start = (bf16[512,256]{1,0:T(8,128)(2,1)S(1)}, bf16[512,256]{1,0:T(8,128)(2,1)S(1)}, u32[]{:S(2)}, u32[]{:S(2)}) collective-permute-start(bf16[512,256]{1,0:T(8,128)(2,1)S(1)} %copy.14), channel_id=1, source_target_pairs={{0,1},{1,2},{2,3},{3,4},{4,5},{5,6},{6,7},{7,8},{8,9},{9,10},{10,1... | collective-permute-start | bytes 786440 | tf_op jit(solution)/shard_map/while/body/eval_jaxpr/ppermute | solution.py:10
  142.4 15.1 %collective-permute-start.1 = (f32[512,256]{1,0:T(8,128)S(1)}, f32[512,256]{1,0:T(8,128)S(1)}, u32[]{:S(2)}, u32[]{:S(2)}) collective-permute-start(f32[512,256]{1,0:T(8,128)S(1)} %convolution_add_fusion.4), channel_id=1, source_target_pairs={{0,1},{1,2},{2,3},{3,4},{4,5},{5,6},{6,7},{7,8},{8,9},{9,10},{10,1... | collective-permute-start | bytes 1572872 | tf_op jit(solution)/shard_map/while/body/eval_jaxpr/ppermute | solution.py:10
  142.5 15.0 %collective-permute-start = (bf16[512,256]{1,0:T(8,128)(2,1)S(1)}, bf16[512,256]{1,0:T(8,128)(2,1)S(1)}, u32[]{:S(2)}, u32[]{:S(2)}) collective-permute-start(bf16[512,256]{1,0:T(8,128)(2,1)S(1)} %copy.14), channel_id=1, source_target_pairs={{0,1},{1,2},{2,3},{3,4},{4,5},{5,6},{6,7},{7,8},{8,9},{9,10},{10,1... | collective-permute-start | bytes 786440 | tf_op jit(solution)/shard_map/while/body/eval_jaxpr/ppermute | solution.py:10
  160.5 15.1 %collective-permute-start.1 = (f32[512,256]{1,0:T(8,128)S(1)}, f32[512,256]{1,0:T(8,128)S(1)}, u32[]{:S(2)}, u32[]{:S(2)}) collective-permute-start(f32[512,256]{1,0:T(8,128)S(1)} %convolution_add_fusion.4), channel_id=1, source_target_pairs={{0,1},{1,2},{2,3},{3,4},{4,5},{5,6},{6,7},{7,8},{8,9},{9,10},{10,1... | collective-permute-start | bytes 1572872 | tf_op jit(solution)/shard_map/while/body/eval_jaxpr/ppermute | solution.py:10
  160.6 15.0 %collective-permute-start = (bf16[512,256]{1,0:T(8,128)(2,1)S(1)}, bf16[512,256]{1,0:T(8,128)(2,1)S(1)}, u32[]{:S(2)}, u32[]{:S(2)}) collective-permute-start(bf16[512,256]{1,0:T(8,128)(2,1)S(1)} %copy.14), channel_id=1, source_target_pairs={{0,1},{1,2},{2,3},{3,4},{4,5},{5,6},{6,7},{7,8},{8,9},{9,10},{10,1... | collective-permute-start | bytes 786440 | tf_op jit(solution)/shard_map/while/body/eval_jaxpr/ppermute | solution.py:10
  178.6 15.1 %collective-permute-start.1 = (f32[512,256]{1,0:T(8,128)S(1)}, f32[512,256]{1,0:T(8,128)S(1)}, u32[]{:S(2)}, u32[]{:S(2)}) collective-permute-start(f32[512,256]{1,0:T(8,128)S(1)} %convolution_add_fusion.4), channel_id=1, source_target_pairs={{0,1},{1,2},{2,3},{3,4},{4,5},{5,6},{6,7},{7,8},{8,9},{9,10},{10,1... | collective-permute-start | bytes 1572872 | tf_op jit(solution)/shard_map/while/body/eval_jaxpr/ppermute | solution.py:10
  178.7 15.0 %collective-permute-start = (bf16[512,256]{1,0:T(8,128)(2,1)S(1)}, bf16[512,256]{1,0:T(8,128)(2,1)S(1)}, u32[]{:S(2)}, u32[]{:S(2)}) collective-permute-start(bf16[512,256]{1,0:T(8,128)(2,1)S(1)} %copy.14), channel_id=1, source_target_pairs={{0,1},{1,2},{2,3},{3,4},{4,5},{5,6},{6,7},{7,8},{8,9},{9,10},{10,1... | collective-permute-start | bytes 786440 | tf_op jit(solution)/shard_map/while/body/eval_jaxpr/ppermute | solution.py:10
  196.7 15.1 %collective-permute-start.1 = (f32[512,256]{1,0:T(8,128)S(1)}, f32[512,256]{1,0:T(8,128)S(1)}, u32[]{:S(2)}, u32[]{:S(2)}) collective-permute-start(f32[512,256]{1,0:T(8,128)S(1)} %convolution_add_fusion.4), channel_id=1, source_target_pairs={{0,1},{1,2},{2,3},{3,4},{4,5},{5,6},{6,7},{7,8},{8,9},{9,10},{10,1... | collective-permute-start | bytes 1572872 | tf_op jit(solution)/shard_map/while/body/eval_jaxpr/ppermute | solution.py:10
  196.8 15.0 %collective-permute-start = (bf16[512,256]{1,0:T(8,128)(2,1)S(1)}, bf16[512,256]{1,0:T(8,128)(2,1)S(1)}, u32[]{:S(2)}, u32[]{:S(2)}) collective-permute-start(bf16[512,256]{1,0:T(8,128)(2,1)S(1)} %copy.14), channel_id=1, source_target_pairs={{0,1},{1,2},{2,3},{3,4},{4,5},{5,6},{6,7},{7,8},{8,9},{9,10},{10,1... | collective-permute-start | bytes 786440 | tf_op jit(solution)/shard_map/while/body/eval_jaxpr/ppermute | solution.py:10
  214.8 15.1 %collective-permute-start.1 = (f32[512,256]{1,0:T(8,128)S(1)}, f32[512,256]{1,0:T(8,128)S(1)}, u32[]{:S(2)}, u32[]{:S(2)}) collective-permute-start(f32[512,256]{1,0:T(8,128)S(1)} %convolution_add_fusion.4), channel_id=1, source_target_pairs={{0,1},{1,2},{2,3},{3,4},{4,5},{5,6},{6,7},{7,8},{8,9},{9,10},{10,1... | collective-permute-start | bytes 1572872 | tf_op jit(solution)/shard_map/while/body/eval_jaxpr/ppermute | solution.py:10
  214.9 15.0 %collective-permute-start = (bf16[512,256]{1,0:T(8,128)(2,1)S(1)}, bf16[512,256]{1,0:T(8,128)(2,1)S(1)}, u32[]{:S(2)}, u32[]{:S(2)}) collective-permute-start(bf16[512,256]{1,0:T(8,128)(2,1)S(1)} %copy.14), channel_id=1, source_target_pairs={{0,1},{1,2},{2,3},{3,4},{4,5},{5,6},{6,7},{7,8},{8,9},{9,10},{10,1... | collective-permute-start | bytes 786440 | tf_op jit(solution)/shard_map/while/body/eval_jaxpr/ppermute | solution.py:10
  232.9 15.1 %collective-permute-start.1 = (f32[512,256]{1,0:T(8,128)S(1)}, f32[512,256]{1,0:T(8,128)S(1)}, u32[]{:S(2)}, u32[]{:S(2)}) collective-permute-start(f32[512,256]{1,0:T(8,128)S(1)} %convolution_add_fusion.4), channel_id=1, source_target_pairs={{0,1},{1,2},{2,3},{3,4},{4,5},{5,6},{6,7},{7,8},{8,9},{9,10},{10,1... | collective-permute-start | bytes 1572872 | tf_op jit(solution)/shard_map/while/body/eval_jaxpr/ppermute | solution.py:10
  233.0 15.0 %collective-permute-start = (bf16[512,256]{1,0:T(8,128)(2,1)S(1)}, bf16[512,256]{1,0:T(8,128)(2,1)S(1)}, u32[]{:S(2)}, u32[]{:S(2)}) collective-permute-start(bf16[512,256]{1,0:T(8,128)(2,1)S(1)} %copy.14), channel_id=1, source_target_pairs={{0,1},{1,2},{2,3},{3,4},{4,5},{5,6},{6,7},{7,8},{8,9},{9,10},{10,1... | collective-permute-start | bytes 786440 | tf_op jit(solution)/shard_map/while/body/eval_jaxpr/ppermute | solution.py:10
  251.0 15.1 %collective-permute-start.1 = (f32[512,256]{1,0:T(8,128)S(1)}, f32[512,256]{1,0:T(8,128)S(1)}, u32[]{:S(2)}, u32[]{:S(2)}) collective-permute-start(f32[512,256]{1,0:T(8,128)S(1)} %convolution_add_fusion.4), channel_id=1, source_target_pairs={{0,1},{1,2},{2,3},{3,4},{4,5},{5,6},{6,7},{7,8},{8,9},{9,10},{10,1... | collective-permute-start | bytes 1572872 | tf_op jit(solution)/shard_map/while/body/eval_jaxpr/ppermute | solution.py:10
  251.1 15.0 %collective-permute-start = (bf16[512,256]{1,0:T(8,128)(2,1)S(1)}, bf16[512,256]{1,0:T(8,128)(2,1)S(1)}, u32[]{:S(2)}, u32[]{:S(2)}) collective-permute-start(bf16[512,256]{1,0:T(8,128)(2,1)S(1)} %copy.14), channel_id=1, source_target_pairs={{0,1},{1,2},{2,3},{3,4},{4,5},{5,6},{6,7},{7,8},{8,9},{9,10},{10,1... | collective-permute-start | bytes 786440 | tf_op jit(solution)/shard_map/while/body/eval_jaxpr/ppermute | solution.py:10
  269.1 15.1 %collective-permute-start.1 = (f32[512,256]{1,0:T(8,128)S(1)}, f32[512,256]{1,0:T(8,128)S(1)}, u32[]{:S(2)}, u32[]{:S(2)}) collective-permute-start(f32[512,256]{1,0:T(8,128)S(1)} %convolution_add_fusion.4), channel_id=1, source_target_pairs={{0,1},{1,2},{2,3},{3,4},{4,5},{5,6},{6,7},{7,8},{8,9},{9,10},{10,1... | collective-permute-start | bytes 1572872 | tf_op jit(solution)/shard_map/while/body/eval_jaxpr/ppermute | solution.py:10
  269.2 15.0 %collective-permute-start = (bf16[512,256]{1,0:T(8,128)(2,1)S(1)}, bf16[512,256]{1,0:T(8,128)(2,1)S(1)}, u32[]{:S(2)}, u32[]{:S(2)}) collective-permute-start(bf16[512,256]{1,0:T(8,128)(2,1)S(1)} %copy.14), channel_id=1, source_target_pairs={{0,1},{1,2},{2,3},{3,4},{4,5},{5,6},{6,7},{7,8},{8,9},{9,10},{10,1... | collective-permute-start | bytes 786440 | tf_op jit(solution)/shard_map/while/body/eval_jaxpr/ppermute | solution.py:10
  287.2 15.1 %collective-permute-start.1 = (f32[512,256]{1,0:T(8,128)S(1)}, f32[512,256]{1,0:T(8,128)S(1)}, u32[]{:S(2)}, u32[]{:S(2)}) collective-permute-start(f32[512,256]{1,0:T(8,128)S(1)} %convolution_add_fusion.4), channel_id=1, source_target_pairs={{0,1},{1,2},{2,3},{3,4},{4,5},{5,6},{6,7},{7,8},{8,9},{9,10},{10,1... | collective-permute-start | bytes 1572872 | tf_op jit(solution)/shard_map/while/body/eval_jaxpr/ppermute | solution.py:10
  287.3 15.0 %collective-permute-start = (bf16[512,256]{1,0:T(8,128)(2,1)S(1)}, bf16[512,256]{1,0:T(8,128)(2,1)S(1)}, u32[]{:S(2)}, u32[]{:S(2)}) collective-permute-start(bf16[512,256]{1,0:T(8,128)(2,1)S(1)} %copy.14), channel_id=1, source_target_pairs={{0,1},{1,2},{2,3},{3,4},{4,5},{5,6},{6,7},{7,8},{8,9},{9,10},{10,1... | collective-permute-start | bytes 786440 | tf_op jit(solution)/shard_map/while/body/eval_jaxpr/ppermute | solution.py:10
  305.3 15.1 %collective-permute-start.1 = (f32[512,256]{1,0:T(8,128)S(1)}, f32[512,256]{1,0:T(8,128)S(1)}, u32[]{:S(2)}, u32[]{:S(2)}) collective-permute-start(f32[512,256]{1,0:T(8,128)S(1)} %convolution_add_fusion.4), channel_id=1, source_target_pairs={{0,1},{1,2},{2,3},{3,4},{4,5},{5,6},{6,7},{7,8},{8,9},{9,10},{10,1... | collective-permute-start | bytes 1572872 | tf_op jit(solution)/shard_map/while/body/eval_jaxpr/ppermute | solution.py:10
  305.4 15.0 %collective-permute-start = (bf16[512,256]{1,0:T(8,128)(2,1)S(1)}, bf16[512,256]{1,0:T(8,128)(2,1)S(1)}, u32[]{:S(2)}, u32[]{:S(2)}) collective-permute-start(bf16[512,256]{1,0:T(8,128)(2,1)S(1)} %copy.14), channel_id=1, source_target_pairs={{0,1},{1,2},{2,3},{3,4},{4,5},{5,6},{6,7},{7,8},{8,9},{9,10},{10,1... | collective-permute-start | bytes 786440 | tf_op jit(solution)/shard_map/while/body/eval_jaxpr/ppermute | solution.py:10
where the time goes:
time: 326 us; the launch traced here: 325 us
  waiting for transfers between devices  232 us (71%)
  matrix products  31.8 us (10%)
  blocking collectives  24.4 us (7%)
  local copies, waits for them, and re-layouts  13 us (4%)
  loops' own time  11.7 us (4%)
  other arithmetic  7.44 us (2%)
    ppermute x32, waiting for transfers between devices, passed_along(): return lax.ppermute(value, axis, pairs)  232 us
    all_gather x1, blocking collectives, on_device(): logz_all = lax.all_gather(target_logzeta_saved, 'blk', axis=0, tiled=True)  24.4 us
    dot_general x16, matrix products, probability_linkage(): lax.dot_general(sphere_anchors, sphere_targets, (((1,), (1,)), ((), ())),...  20.2 us
    another operation x1, loops' own time, on_device(): lax.scan(visit, (scaled_target_vectors, zeros_rows, zeros_rows), jnp.aran...  11.7 us
    dynamic_slice x16, local copies, waits for them, and re-layouts, on_device(): lax.scan(visit, (scaled_target_vectors, zeros_rows, zeros_rows), jnp.aran...  9.34 us
  transfers between devices with their start and end apart: 32, of which 16 were waited for; matrix products, arithmetic and copies ran while one was open for 2% of the time, Pallas kernels for 0%

commit v1 on v0

v1 whole, which is shorter than its diff:
```python
import functools
import math

import jax
import jax.numpy as jnp
from jax import lax
from jax.experimental import pallas as pl
from jax.experimental.pallas import tpu as pltpu
from jax.sharding import PartitionSpec as P

MESH = pl.DeviceIdType.MESH
BF, F32 = jnp.bfloat16, jnp.float32
NT = (((1,), (1,)), ((), ()))


def unit_rows(block):
    floats = block.astype(F32)
    inverse = lax.rsqrt(jnp.sum(floats * floats, axis=1, keepdims=True) + 1e-06)
    return inverse, floats * inverse


def exchange_kernel(
    a_hbm, b_hbm, match_hbm, la_hbm, lb_hbm, heat, which,
    da_own, da_left, da_right, db_own, db_core, db_far,
    a_raw, b_raw, match_raw, la_raw, lb_raw,
    ua, uat, ub, aux, eb, ea_col, match_col, da, db, da_out, opp_in, db_out, core_in,
    in_sem, ga_send, ga_recv, gb_send, gb_recv, ra_send, ra_recv, rb_send, rb_recv,
):
    rows = a_hbm.shape[0]
    half = rows // 2
    grp, blk = lax.axis_index("grp"), lax.axis_index("blk")
    x, y, core = blk // 4, (blk // 2) % 2, blk % 2

    def at(px, py, pc):
        return (grp, px * 4 + py * 2 + pc)

    left, right = at((x + 3) % 4, y, core), at((x + 1) % 4, y, core)
    other, far = at(x, y, 1 - core), at(x, 1 - y, core)

    barrier = pltpu.get_barrier_semaphore()
    for peer in (left, right, other, far):
        pl.semaphore_signal(barrier, inc=1, device_id=peer, device_id_type=MESH)

    loads = [
        pltpu.make_async_copy(src, dst, in_sem.at[k])
        for k, (src, dst) in enumerate(
            ((a_hbm, a_raw), (b_hbm, b_raw), (match_hbm, match_raw), (la_hbm, la_raw), (lb_hbm, lb_raw))
        )
    ]
    for load in loads:
        load.start()

    temperature = jnp.float32(0.0)
    for k in range(heat.shape[0]):
        temperature += jnp.where(which[0] == k, heat[k], 0.0)
    scale = math.log2(math.e) / jnp.broadcast_to(temperature, (1, 1))

    def send(src, dst, send_sem, recv_sem, peer):
        copy = pltpu.make_async_remote_copy(
            src_ref=src, dst_ref=dst, send_sem=send_sem, recv_sem=recv_sem, device_id=peer, device_id_type=MESH
        )
        copy.start()
        return copy

    for load in loads:
        load.wait()
    aux[0, 0:4, :] = jnp.exp(-la_raw[...])
    aux[0, 4:8, :] = match_raw[...].astype(F32)
    eb[0] = jnp.exp(-lb_raw[...])
    ua[0] = unit_rows(a_raw[...])[1].astype(BF)
    ub[0] = unit_rows(b_raw[...])[1].astype(BF)

    block_of = (blk, blk - core + 1 - core, blk + 2 - 4 * y, blk + 2 - 4 * y - core + 1 - core)

    def spread(group, part, source):
        columns = aux[source].T
        for k in range(4):
            if k // 2 in part:
                into = pl.ds(k * 128, 128)
                ea_col[group, into, :] = jnp.broadcast_to(columns[:, k : k + 1], (128, 128))
                match_col[group, into, :] = jnp.broadcast_to(columns[:, 4 + k : 5 + k], (128, 128))

    def scores(group, j):
        raw = lax.dot_general(ua[group], ub[j], NT, preferred_element_type=F32)
        chance = jnp.exp2(raw * scale)
        ids = (lax.broadcasted_iota(jnp.int32, (1, rows), 1) + block_of[j] * rows).astype(F32)
        reps = rows // 128
        weight = jnp.concatenate([ea_col[group]] * reps, axis=1) + eb[j]
        paired = jnp.concatenate([match_col[group]] * reps, axis=1) == ids
        value = chance * weight
        return jnp.where(paired, value - 2.0, value).astype(BF)

    def pair(group, j, first_of_group, first_of_j):
        coupling = scores(group, j)
        rows_term = jnp.dot(coupling, ub[j], preferred_element_type=F32)
        columns_term = jnp.dot(uat[group], coupling, preferred_element_type=F32)
        into = da_own if group == 0 else da.at[group - 1]
        if first_of_group:
            into[...] = rows_term
        else:
            into[...] += rows_term
        into = db_own if j == 0 else db.at[j - 1]
        if first_of_j:
            into[...] = columns_term
        else:
            into[...] += columns_term

    uat[0] = ua[0].T
    spread(0, (0, 1), 0)
    pair(0, 0, True, True)

    pl.semaphore_wait(barrier, 4)

    first, second = pl.ds(0, half), pl.ds(half, half)
    aux_right = send(aux.at[0], aux.at[1], ga_send.at[0], ga_recv.at[0], right)
    aux_left = send(aux.at[0], aux.at[2], ga_send.at[1], ga_recv.at[1], left)
    early_right = send(ua.at[0, first], ua.at[1, first], ga_send.at[2], ga_recv.at[2], right)
    early_left = send(ua.at[0, second], ua.at[1, second], ga_send.at[3], ga_recv.at[3], left)
    eb_other = send(eb.at[0], eb.at[1], gb_send.at[0], gb_recv.at[0], other)
    eb_far = send(eb.at[0], eb.at[2], gb_send.at[1], gb_recv.at[1], far)
    b_other = send(ub.at[0], ub.at[1], gb_send.at[2], gb_recv.at[2], other)
    b_far = send(ub.at[0], ub.at[2], gb_send.at[3], gb_recv.at[3], far)

    eb_other.wait_recv()
    b_other.wait_recv()
    pair(0, 1, False, True)

    aux_right.wait_recv()
    aux_left.wait_recv()
    aux_on = send(aux.at[1], aux.at[3], ga_send.at[4], ga_recv.at[4], right)
    early_right.wait_recv()
    opp_right = send(ua.at[1, first], ua.at[2, first], ga_send.at[5], ga_recv.at[5], right)
    early_left.wait_recv()
    opp_left = send(ua.at[1, second], ua.at[2, second], ga_send.at[6], ga_recv.at[6], left)
    late_left = send(ua.at[0, first], ua.at[3, second], ga_send.at[7], ga_recv.at[7], left)
    late_right = send(ua.at[0, second], ua.at[3, first], ga_send.at[8], ga_recv.at[8], right)

    uat[1] = ua[1].T
    spread(1, (0,), 1)
    spread(1, (1,), 2)
    pair(1, 0, True, False)
    pair(1, 1, False, False)

    eb_far.wait_recv()
    eb_on = send(eb.at[2], eb.at[3], gb_send.at[4], gb_recv.at[4], other)
    b_far.wait_recv()
    b_on = send(ub.at[2], ub.at[3], gb_send.at[5], gb_recv.at[5], other)

    aux_on.wait_recv()
    opp_right.wait_recv()
    opp_left.wait_recv()
    uat[2] = ua[2].T
    spread(2, (0, 1), 3)
    pair(2, 0, True, False)
    pair(2, 1, False, False)
    pair(2, 2, False, True)
    eb_on.wait_recv()
    b_on.wait_recv()
    pair(2, 3, False, True)

    da_out[1] = da[1].astype(BF)
    part_right = send(da_out.at[1, first], opp_in.at[first], ra_send.at[0], ra_recv.at[0], right)
    part_left = send(da_out.at[1, second], opp_in.at[second], ra_send.at[1], ra_recv.at[1], left)

    pair(1, 2, False, False)
    pair(1, 3, False, False)
    da_out[0] = da[0].astype(BF)
    sum_left = send(da_out.at[0, first], da_right.at[first], ra_send.at[2], ra_recv.at[2], left)
    sum_right = send(da_out.at[0, second], da_left.at[second], ra_send.at[3], ra_recv.at[3], right)

    pair(0, 2, False, False)
    pair(0, 3, False, False)

    late_left.wait_recv()
    late_right.wait_recv()
    uat[3] = ua[3].T
    columns_left, columns_right = aux[1].T, aux[2].T
    for k in range(4):
        columns = columns_left if k < 2 else columns_right
        kk = (k + 2) % 4
        into = pl.ds(k * 128, 128)
        ea_col[3, into, :] = jnp.broadcast_to(columns[:, kk : kk + 1], (128, 128))
        match_col[3, into, :] = jnp.broadcast_to(columns[:, 4 + kk : 5 + kk], (128, 128))
    pair(3, 3, True, False)
    db_out[2] = db[2].astype(BF)
    core_on = send(db_out.at[2], core_in, rb_send.at[0], rb_recv.at[0], other)
    pair(3, 2, False, False)
    core_on.wait_recv()
    db_out[1] = (db[1] + core_in[...].astype(F32)).astype(BF)
    sum_far = send(db_out.at[1], db_far, rb_send.at[1], rb_recv.at[1], far)
    pair(3, 1, False, False)
    db_out[0] = db[0].astype(BF)
    sum_other = send(db_out.at[0], db_core, rb_send.at[2], rb_recv.at[2], other)
    pair(3, 0, False, False)

    part_right.wait_recv()
    part_left.wait_recv()
    da_out[2, 0:half, :] = (da[2, 0:half, :] + opp_in[half:rows, :].astype(F32)).astype(BF)
    da_out[2, half:rows, :] = (da[2, half:rows, :] + opp_in[0:half, :].astype(F32)).astype(BF)
    last_left = send(da_out.at[2, first], da_right.at[second], ra_send.at[4], ra_recv.at[4], left)
    last_right = send(da_out.at[2, second], da_left.at[first], ra_send.at[5], ra_recv.at[5], right)

    sum_left.wait_recv()
    sum_right.wait_recv()
    sum_other.wait_recv()
    last_left.wait_recv()
    last_right.wait_recv()
    sum_far.wait_recv()
    for copy in (
        aux_right, aux_left, early_right, early_left, aux_on, opp_right, opp_left, late_left, late_right,
        eb_other, eb_far, b_other, b_far, eb_on, b_on,
        part_right, part_left, sum_left, sum_right, last_left, last_right, core_on, sum_far, sum_other,
    ):
        copy.wait_send()


def finish_kernel(a, b, heat, which, da_own, da_left, da_right, db_own, db_core, db_far, out_a, out_b):
    temperature = jnp.float32(0.0)
    for k in range(heat.shape[0]):
        temperature += jnp.where(which[0] == k, heat[k], 0.0)
    scale = 1.0 / jnp.broadcast_to(temperature, (1, 1))

    def tangent(block, total):
        inverse, unit = unit_rows(block)
        dunit = total * scale
        return inverse * (dunit - unit * jnp.sum(unit * dunit, axis=1, keepdims=True))

    total_a = da_own[...] + da_left[...].astype(F32) + da_right[...].astype(F32)
    out_a[...] = tangent(a[...], total_a)
    total_b = db_own[...] + db_core[...].astype(F32) + db_far[...].astype(F32)
    out_b[...] = tangent(b[...], total_b.T)


def on_device(encoded_anchor, encoded_target, matched_target, anchor_logzeta, target_logzeta_saved, heat_values, matchup_position):
    rows, width = encoded_anchor.shape
    half = rows // 2
    anywhere = pl.BlockSpec(memory_space=pl.ANY)
    smem = pl.BlockSpec(memory_space=pltpu.SMEM)
    vmem = pl.BlockSpec(memory_space=pltpu.VMEM)
    dma = pltpu.SemaphoreType.DMA
    pieces = pl.pallas_call(
        exchange_kernel,
        out_shape=(
            jax.ShapeDtypeStruct((rows, width), F32),
            jax.ShapeDtypeStruct((rows, width), BF),
            jax.ShapeDtypeStruct((rows, width), BF),
            jax.ShapeDtypeStruct((width, rows), F32),
            jax.ShapeDtypeStruct((width, rows), BF),
            jax.ShapeDtypeStruct((width, rows), BF),
        ),
        in_specs=[anywhere] * 5 + [smem] * 2,
        out_specs=[vmem] * 6,
        scratch_shapes=[
            pltpu.VMEM((rows, width), BF),
            pltpu.VMEM((rows, width), BF),
            pltpu.VMEM((4, 128), jnp.int32),
            pltpu.VMEM((4, 128), F32),
            pltpu.VMEM((1, rows), F32),
            pltpu.VMEM((4, rows, width), BF),
            pltpu.VMEM((4, width, rows), BF),
            pltpu.VMEM((4, rows, width), BF),
            pltpu.VMEM((4, 8, 128), F32),
            pltpu.VMEM((4, 1, rows), F32),
            pltpu.VMEM((4, rows, 128), F32),
            pltpu.VMEM((4, rows, 128), F32),
            pltpu.VMEM((3, rows, width), F32),
            pltpu.VMEM((3, width, rows), F32),
            pltpu.VMEM((3, rows, width), BF),
            pltpu.VMEM((rows, width), BF),
            pltpu.VMEM((3, width, rows), BF),
            pltpu.VMEM((width, rows), BF),
            dma((5,)),
            dma((9,)),
            dma((9,)),
            dma((6,)),
            dma((6,)),
            dma((6,)),
            dma((6,)),
            dma((3,)),
            dma((3,)),
        ],
        compiler_params=pltpu.CompilerParams(collective_id=7, has_side_effects=True, vmem_limit_bytes=44 << 20),
    )(
        encoded_anchor,
        encoded_target,
        matched_target.reshape(4, 128),
        anchor_logzeta.reshape(4, 128),
        target_logzeta_saved.reshape(1, rows),
        heat_values,
        matchup_position,
    )
    return pl.pallas_call(
        finish_kernel,
        out_shape=(jax.ShapeDtypeStruct((rows, width), F32), jax.ShapeDtypeStruct((rows, width), F32)),
        in_specs=[vmem] * 2 + [smem] * 2 + [vmem] * 6,
        out_specs=[vmem] * 2,
        compiler_params=pltpu.CompilerParams(vmem_limit_bytes=32 << 20),
    )(encoded_anchor, encoded_target, heat_values, matchup_position, *pieces)


def solution(mesh):
    both = ("grp", "blk")
    return jax.shard_map(
        on_device,
        mesh=mesh,
        in_specs=(P(both, None), P(both, None), P(both), P(both), P(both), P("grp"), P("grp")),
        out_specs=(P(both, None), P(both, None)),
        check_vma=False,
    )
```

time: 326 us -> 37 us (0.11)
  the two profiles are of different devices: /device:TPU:128 before, /device:TPU:1 now
where the time goes in v1:
time: 37 us; the launch traced here: 36.9 us
  Pallas kernels  32.9 us (89%)
  local copies, waits for them, and re-layouts  2.57 us (7%)
  between operations  1.34 us (4%)
    pallas_call x1, Pallas kernels, on_device(): pl.pallas_call(exchange_kernel, out_shape=(jax.ShapeDtypeStruct((rows, wi...  31 us
    unnamed x12, local copies, waits for them, and re-layouts  2.57 us
    pallas_call x1, Pallas kernels, on_device(): pl.pallas_call(finish_kernel, out_shape=(jax.ShapeDtypeStruct((rows, widt...  1.94 us

profile of v1, /device:TPU:1, one launch (start us, length us, event | category | flops | bytes accessed | tf_op | source)
XLA Modules:
  0.0 36.9 jit_solution(13307024656327710010)
XLA Ops:
  0.6 0.0 copy-start.4
  1.3 0.0 copy-start.3
  1.3 0.0 copy-start.2
  1.3 0.0 copy-start.5
  1.3 0.0 copy-done.4
  1.3 0.6 %copy-done.3 = f32[512]{0:T(512)S(1)} copy-done((f32[512]{0:T(512)S(1)}, f32[512]{0:T(512)}, u32[]{:S(2)}) %copy-start.3) | copy-done | bytes 2072
  2.0 0.0 copy-done.2
  2.0 0.0 copy-done.5
  2.0 0.0 copy-start
  2.0 0.9 %copy-done = bf16[512,256]{1,0:T(8,128)(2,1)S(1)} copy-done((bf16[512,256]{1,0:T(8,128)(2,1)S(1)}, bf16[512,256]{1,0:T(8,128)(2,1)}, u32[]{:S(2)}) %copy-start) | copy-done | bytes 262168
  3.0 0.0 copy-start.1
  3.0 0.9 %copy-done.1 = bf16[512,256]{1,0:T(8,128)(2,1)S(1)} copy-done((bf16[512,256]{1,0:T(8,128)(2,1)S(1)}, bf16[512,256]{1,0:T(8,128)(2,1)}, u32[]{:S(2)}) %copy-start.1) | copy-done | bytes 262168
  3.9 31.0 %shard_map.86 = (f32[512,256]{1,0:T(8,128)S(1)}, bf16[512,256]{1,0:T(8,128)(2,1)S(1)}, bf16[512,256]{1,0:T(8,128)(2,1)S(1)}, f32[256,512]{1,0:T(8,128)S(1)}, bf1...) custom-call(bf16[512,256]{1,0:T(8,128)(2,1)S(1)} %copy-done, bf16[512,256]{1,0:T(8,128)(2,1)S(1)} %copy-done.1, ...), custom_call_target="tpu_custom_call" | custom-call | tf_op jit(solution)/shard_map/pallas_call | solution.py:241
  34.9 1.9 %shard_map.87 = (f32[512,256]{1,0:T(8,128)}, f32[512,256]{1,0:T(8,128)}) custom-call(bf16[512,256]{1,0:T(8,128)(2,1)S(1)} %copy-done, bf16[512,256]{1,0:T(8,128)(2,1)S(1)} %copy-done.1, f32[4]{0:T(128)S(1)} %copy-done.5, s32[1]{0:T(128)S(6)} %copy.9.which, f32[512,256]{1,0:T(8,128)S(1)} %get-tuple-element.8.da_own, ...), custom_call_target="tpu_custom_call" | custom-call | tf_op jit(solution)/shard_map/pallas_call | solution.py:292
Async XLA Ops:
  0.6 0.7 %copy-start.4 = (f32[512]{0:T(512)S(1)}, f32[512]{0:T(512)}, u32[]{:S(2)}) copy-start(f32[512]{0:T(512)} %param.11) | copy-start | bytes 6148
  1.3 0.7 %copy-start.3 = (f32[512]{0:T(512)S(1)}, f32[512]{0:T(512)}, u32[]{:S(2)}) copy-start(f32[512]{0:T(512)} %param.10) | copy-start | bytes 6148
  1.3 0.7 %copy-start.2 = (s32[512]{0:T(512)S(1)}, s32[512]{0:T(512)}, u32[]{:S(2)}) copy-start(s32[512]{0:T(512)} %param.9) | copy-start | bytes 6148
  1.3 0.7 %copy-start.5 = (f32[4]{0:T(128)S(1)}, f32[4]{0:T(128)}, u32[]{:S(2)}) copy-start(f32[4]{0:T(128)} %heat.3) | copy-start | bytes 52
  2.0 1.0 %copy-start = (bf16[512,256]{1,0:T(8,128)(2,1)S(1)}, bf16[512,256]{1,0:T(8,128)(2,1)}, u32[]{:S(2)}) copy-start(bf16[512,256]{1,0:T(8,128)(2,1)} %a.1) | copy-start | bytes 786436
  3.0 0.9 %copy-start.1 = (bf16[512,256]{1,0:T(8,128)(2,1)S(1)}, bf16[512,256]{1,0:T(8,128)(2,1)}, u32[]{:S(2)}) copy-start(bf16[512,256]{1,0:T(8,128)(2,1)} %b.1) | copy-start | bytes 786436

commit v2 on v0

v2 whole, which is shorter than its diff:
```python
import functools
import math

import jax
import jax.numpy as jnp
from jax import lax
from jax.experimental import pallas as pl
from jax.experimental.pallas import tpu as pltpu
from jax.sharding import PartitionSpec as P

MESH = pl.DeviceIdType.MESH
BF, F32 = jnp.bfloat16, jnp.float32
NT = (((1,), (1,)), ((), ()))
TN = (((0,), (0,)), ((), ()))


def unit_rows(block):
    floats = block.astype(F32)
    inverse = lax.rsqrt(jnp.sum(floats * floats, axis=1, keepdims=True) + 1e-06)
    return inverse, floats * inverse


def exchange_kernel(
    a_hbm, b_hbm, match_hbm, la_hbm, lb_hbm, heat_hbm, which,
    scale_out, a_own, b_own, da_own, da_left, da_right, db_own, db_core, db_far,
    a_in, b_in, ua, ub, match, la, lb, eb, ids, ea_col, match_col, da, db, da_out, opp_in, db_out, db_other, core_in, heat,
    in_sem, send_sems, recv_sems,
):
    rows = a_hbm.shape[0]
    half, quarter = rows // 2, rows // 4
    first, second = pl.ds(0, half), pl.ds(half, half)
    grp, blk = lax.axis_index("grp"), lax.axis_index("blk")
    x, y, core = blk // 4, (blk // 2) % 2, blk % 2

    def at(px, py, pc):
        return px * 4 + py * 2 + pc

    left, right = at((x + 3) % 4, y, core), at((x + 1) % 4, y, core)
    other, far, far_other = at(x, y, 1 - core), at(x, 1 - y, core), at(x, 1 - y, 1 - core)

    barrier = pltpu.get_barrier_semaphore()
    for peer in (left, right, other, far):
        pl.semaphore_signal(barrier, inc=1, device_id=(grp, peer), device_id_type=MESH)

    loads = [
        pltpu.make_async_copy(src, dst, in_sem.at[k])
        for k, (src, dst) in enumerate(
            ((a_hbm, a_own), (b_hbm, b_own), (match_hbm, match.at[0]), (la_hbm, la.at[0]), (lb_hbm, lb.at[0]),
             (heat_hbm, heat))
        )
    ]
    for load in loads:
        load.start()

    copies = []

    def send(src, dst, peer):
        k = len(copies)
        copy = pltpu.make_async_remote_copy(
            src_ref=src, dst_ref=dst, send_sem=send_sems.at[k], recv_sem=recv_sems.at[k],
            device_id=(grp, peer), device_id_type=MESH,
        )
        copy.start()
        copies.append(copy)
        return copy

    def take_a(group, pieces):
        ua[group] = unit_rows(a_own[...] if group == 0 else a_in[group - 1])[1].astype(BF)
        columns = {}
        for source in sorted({source for source, _ in pieces}):
            columns[source] = (jnp.exp(-la[source]).T, match[source].astype(F32).T)
        for k, (source, quarter) in enumerate(pieces):
            into = pl.ds(k * 128, 128)
            weights, partners = columns[source]
            ea_col[group, into, :] = jnp.broadcast_to(weights[:, quarter : quarter + 1], (128, 128))
            match_col[group, into, :] = jnp.broadcast_to(partners[:, quarter : quarter + 1], (128, 128))

    def take_b(j):
        ub[j] = unit_rows(b_own[...] if j == 0 else b_in[j - 1])[1].astype(BF)
        along = lax.broadcasted_iota(jnp.int32, (1, rows), 1)
        if j < 2:
            eb[j] = jnp.exp(-lb[j])
            numbers = along + (blk, other)[j] * rows
        else:
            part = slice(0, half) if j == 2 else slice(half, rows)
            eb[j] = jnp.exp(-jnp.concatenate([lb[2][:, part], lb[3][:, part]], axis=1))
            begin = (j - 2) * half
            numbers = jnp.where(along < half, along + (far * rows + begin), along + (far_other * rows + begin - half))
        ids[j] = numbers.astype(F32)

    begun = set()

    def add(into, term, key):
        if key in begun:
            into[...] += term
        else:
            into[...] = term
        begun.add(key)

    def raw_scores(group, j):
        return lax.dot_general(ua[group], ub[j], NT, preferred_element_type=F32)

    def spend(raw, group, j):
        chance = jnp.exp2(raw * scale)
        reps = rows // 128
        weight = jnp.concatenate([ea_col[group]] * reps, axis=1) + eb[j]
        paired = jnp.concatenate([match_col[group]] * reps, axis=1) == ids[j]
        value = chance * weight
        coupling = jnp.where(paired, value - 2.0, value).astype(BF)
        rows_term = jnp.dot(coupling, ub[j], preferred_element_type=F32)
        add(da_own if group == 0 else da.at[group - 1], rows_term, ("a", group))
        columns_term = lax.dot_general(coupling, ua[group], TN, preferred_element_type=F32)
        add(db_own if j == 0 else db.at[j - 1], columns_term, ("b", j))

    def pairs(*todo):
        ahead = raw_scores(*todo[0])
        for k, (group, j) in enumerate(todo):
            raw = ahead
            if k + 1 < len(todo):
                ahead = raw_scores(*todo[k + 1])
            spend(raw, group, j)

    pl.semaphore_wait(barrier, 4)
    quarters = [pl.ds(k * quarter, quarter) for k in range(4)]
    early_right = [send(a_hbm.at[quarters[k]], a_in.at[0, quarters[k]], right) for k in (0, 1)]
    early_left = [send(a_hbm.at[quarters[k]], a_in.at[0, quarters[k]], left) for k in (2, 3)]
    b_other = send(b_hbm, b_in.at[0], other)
    far_a = send(b_hbm.at[first], b_in.at[1, first], far)
    small_left = [send(match_hbm, match.at[2], left), send(la_hbm, la.at[2], left)]
    small_right = [send(match_hbm, match.at[1], right), send(la_hbm, la.at[1], right)]
    lb_other = send(lb_hbm, lb.at[1], other)
    lb_far = send(lb_hbm, lb.at[2], far)
    late_left = send(a_hbm.at[first], a_in.at[2, second], left)
    late_right = send(a_hbm.at[second], a_in.at[2, first], right)

    for load in loads:
        load.wait()
    temperature = jnp.float32(0.0)
    for k in range(heat.shape[0]):
        temperature += jnp.where(which[0] == k, heat[k], 0.0)
    scale = math.log2(math.e) / jnp.broadcast_to(temperature, (1, 1))
    scale_out[...] = jnp.broadcast_to(1.0 / jnp.broadcast_to(temperature, (1, 1)), (8, 128))
    take_a(0, [(0, 0), (0, 1), (0, 2), (0, 3)])
    take_b(0)
    pairs((0, 0))

    opp = []
    for k in (0, 1):
        early_right[k].wait_recv()
        opp.append(send(a_in.at[0, quarters[k]], a_in.at[1, quarters[k]], right))
        early_left[k].wait_recv()
        opp.append(send(a_in.at[0, quarters[k + 2]], a_in.at[1, quarters[k + 2]], left))
    far_b = send(b_hbm.at[second], b_in.at[2, first], far)
    for copy in small_left + small_right:
        copy.wait_recv()
    small_on = [send(match.at[1], match.at[3], right), send(la.at[1], la.at[3], right)]
    lb_far.wait_recv()
    lb_on = send(lb.at[2], lb.at[3], other)
    b_other.wait_recv()
    lb_other.wait_recv()

    take_b(1)
    take_a(1, [(1, 0), (1, 1), (2, 2), (2, 3)])
    pairs((0, 1), (1, 0), (1, 1))

    far_a.wait_recv()
    far_a_on = send(b_in.at[1, first], b_in.at[1, second], other)
    lb_on.wait_recv()
    far_a_on.wait_recv()
    take_b(2)
    pairs((0, 2), (1, 2))

    far_b.wait_recv()
    far_b_on = send(b_in.at[2, first], b_in.at[2, second], other)
    for copy in small_on + opp:
        copy.wait_recv()
    take_a(2, [(3, 0), (3, 1), (3, 2), (3, 3)])
    pairs((2, 0), (2, 1))

    far_b_on.wait_recv()
    take_b(3)
    pairs((2, 2), (2, 3))
    da_out[1] = da[1].astype(BF)
    part_right = send(da_out.at[1, first], opp_in.at[first], right)
    part_left = send(da_out.at[1, second], opp_in.at[second], left)

    late_left.wait_recv()
    late_right.wait_recv()
    take_a(3, [(1, 2), (1, 3), (2, 0), (2, 1)])
    pairs((3, 2), (1, 3))
    db_out[0] = db[1, half:rows].astype(BF)
    core_a = send(db_out.at[0], core_in.at[0], other)
    da_out[0] = da[0].astype(BF)
    sum_left = send(da_out.at[0, first], da_right.at[first], left)
    sum_right = send(da_out.at[0, second], da_left.at[second], right)

    pairs((0, 3), (3, 3))
    db_out[1] = db[2, half:rows].astype(BF)
    core_b = send(db_out.at[1], core_in.at[1], other)
    core_a.wait_recv()
    db_out[2] = (db[1, 0:half] + core_in[0].astype(F32)).astype(BF)
    sum_far_a = send(db_out.at[2], db_far.at[first], far)

    pairs((3, 1), (3, 0))
    core_b.wait_recv()
    db_out[3] = (db[2, 0:half] + core_in[1].astype(F32)).astype(BF)
    sum_far_b = send(db_out.at[3], db_far.at[second], far)
    db_other[...] = db[0].astype(BF)
    sum_other = send(db_other, db_core, other)

    part_right.wait_recv()
    part_left.wait_recv()
    da_out[2, 0:half, :] = (da[2, 0:half, :] + opp_in[half:rows, :].astype(F32)).astype(BF)
    da_out[2, half:rows, :] = (da[2, half:rows, :] + opp_in[0:half, :].astype(F32)).astype(BF)
    last_left = send(da_out.at[2, first], da_right.at[second], left)
    last_right = send(da_out.at[2, second], da_left.at[first], right)

    for copy in (sum_left, sum_right, sum_other, sum_far_a, last_left, last_right, sum_far_b):
        copy.wait_recv()
    for copy in copies:
        copy.wait_send()


def finish_kernel(
    scale, a, b, da_own, da_left, da_right, db_own, db_core, db_far, out_a, out_b, result, sems
):
    rows = a.shape[0]
    half = rows // 2
    by_temperature = scale[0:1, 0:1]

    def tangent(block, total):
        inverse, unit = unit_rows(block)
        dunit = total * by_temperature
        return inverse * (dunit - unit * jnp.sum(unit * dunit, axis=1, keepdims=True))

    copies = []
    for which, (block, total, parts, out) in enumerate(
        ((b, db_own, (db_core, db_far), out_b), (a, da_own, (da_left, da_right), out_a))
    ):
        for k in range(2):
            part = pl.ds(k * half, half)
            summed = total[part] + parts[0][part].astype(F32) + parts[1][part].astype(F32)
            result[which, part] = tangent(block[part], summed)
            copies.append(pltpu.make_async_copy(result.at[which, part], out.at[part], sems.at[2 * which + k]))
            copies[-1].start()
    for copy in copies:
        copy.wait()


def on_device(encoded_anchor, encoded_target, matched_target, anchor_logzeta, target_logzeta_saved, heat_values, matchup_position):
    rows, width = encoded_anchor.shape
    anywhere = pl.BlockSpec(memory_space=pl.ANY)
    vmem = pl.BlockSpec(memory_space=pltpu.VMEM)
    dma = pltpu.SemaphoreType.DMA
    block = jax.ShapeDtypeStruct((rows, width), BF)
    pieces = pl.pallas_call(
        exchange_kernel,
        out_shape=(
            jax.ShapeDtypeStruct((8, 128), F32),
            block,
            block,
            jax.ShapeDtypeStruct((rows, width), F32),
            block,
            block,
            jax.ShapeDtypeStruct((rows, width), F32),
            block,
            block,
        ),
        in_specs=[anywhere] * 6 + [pl.BlockSpec(memory_space=pltpu.SMEM)],
        out_specs=[vmem] * 9,
        scratch_shapes=[
            pltpu.VMEM((3, rows, width), BF),
            pltpu.VMEM((3, rows, width), BF),
            pltpu.VMEM((4, rows, width), BF),
            pltpu.VMEM((4, rows, width), BF),
            pltpu.VMEM((4, 4, 128), jnp.int32),
            pltpu.VMEM((4, 4, 128), F32),
            pltpu.VMEM((4, 1, rows), F32),
            pltpu.VMEM((4, 1, rows), F32),
            pltpu.VMEM((4, 1, rows), F32),
            pltpu.VMEM((4, rows, 128), F32),
            pltpu.VMEM((4, rows, 128), F32),
            pltpu.VMEM((3, rows, width), F32),
            pltpu.VMEM((3, rows, width), F32),
            pltpu.VMEM((3, rows, width), BF),
            pltpu.VMEM((rows, width), BF),
            pltpu.VMEM((4, rows // 2, width), BF),
            pltpu.VMEM((rows, width), BF),
            pltpu.VMEM((2, rows // 2, width), BF),
            pltpu.SMEM((4,), F32),
            dma((6,)),
            dma((36,)),
            dma((36,)),
        ],
        compiler_params=pltpu.CompilerParams(collective_id=7, has_side_effects=True, vmem_limit_bytes=44 << 20),
    )(
        *(
            pltpu.with_memory_space_constraint(value, pltpu.HBM)
            for value in (
                encoded_anchor,
                encoded_target,
                matched_target.reshape(4, 128),
                anchor_logzeta.reshape(4, 128),
                target_logzeta_saved.reshape(1, rows),
                heat_values,
            )
        ),
        matchup_position,
    )
    return pl.pallas_call(
        finish_kernel,
        out_shape=(jax.ShapeDtypeStruct((rows, width), F32), jax.ShapeDtypeStruct((rows, width), F32)),
        in_specs=[vmem] * 9,
        out_specs=[anywhere] * 2,
        scratch_shapes=[pltpu.VMEM((2, rows, width), F32), dma((4,))],
        compiler_params=pltpu.CompilerParams(vmem_limit_bytes=32 << 20),
    )(*pieces)


def solution(mesh):
    both = ("grp", "blk")
    return jax.shard_map(
        on_device,
        mesh=mesh,
        in_specs=(P(both, None), P(both, None), P(both), P(both), P(both), P("grp"), P("grp")),
        out_specs=(P(both, None), P(both, None)),
        check_vma=False,
    )
```

time: 326 us -> 33.4 us (0.10)
  the two profiles are of different devices: /device:TPU:128 before, /device:TPU:1 now
where the time goes in v2:
time: 33.4 us; the launch traced here: 33.3 us
  Pallas kernels  32 us (96%)
  between operations  1.29 us (4%)
    pallas_call x1, Pallas kernels, on_device(): pl.pallas_call(exchange_kernel, out_shape=(jax.ShapeDtypeStruct((8, 128),...  30.6 us
    pallas_call x1, Pallas kernels, on_device(): pl.pallas_call(finish_kernel, out_shape=(jax.ShapeDtypeStruct((rows, widt...  1.33 us

profile of v2, /device:TPU:1, one launch (start us, length us, event | category | flops | bytes accessed | tf_op | source)
XLA Modules:
  0.0 33.3 jit_solution(7406608837540577985)
XLA Ops:
  1.3 30.6 %shard_map.86 = (f32[8,128]{1,0:T(8,128)S(1)}, bf16[512,256]{1,0:T(8,128)(2,1)S(1)}, bf16[512,256]{1,0:T(8,128)(2,1)S(1)}, f32[512,256]{1,0:T(8,128)S(1)}, bf16[...) custom-call(bf16[512,256]{1,0:T(8,128)(2,1)} %a_hbm.1, ...), custom_call_target="tpu_custom_call" | custom-call | tf_op jit(solution)/shard_map/pallas_call | solution.py:256
  31.9 1.3 %shard_map.87 = (f32[512,256]{1,0:T(8,128)}, f32[512,256]{1,0:T(8,128)}) custom-call(f32[8,128]{1,0:T(8,128)S(1)} %get-tuple-element.11.scale, bf16[512,256]{1,0:T(8,128)(2,1)S(1)} %get-tuple-element.12.a, bf16[512,256]{1,0:T(8,128)(2,1)S(1)} %get-tuple-element.13.b, f32[512,256]{1,0:T(8,128)S(1)} %get-tuple-element.14.da_own, ...), custom_call_target="tpu_custom_call" | custom-call | tf_op jit(solution)/shard_map/pallas_call | solution.py:310

commit v3 on v2

--- a/solution.py
+++ b/solution.py
@@ -75,18 +75,16 @@
             ea_col[group, into, :] = jnp.broadcast_to(weights[:, quarter : quarter + 1], (128, 128))
             match_col[group, into, :] = jnp.broadcast_to(partners[:, quarter : quarter + 1], (128, 128))
 
-    def take_b(j):
-        ub[j] = unit_rows(b_own[...] if j == 0 else b_in[j - 1])[1].astype(BF)
-        along = lax.broadcasted_iota(jnp.int32, (1, rows), 1)
+    def take_b(j, part):
+        into = pl.ds(part * half, half)
+        ub[j, into] = unit_rows((b_own if j == 0 else b_in.at[j - 1])[into])[1].astype(BF)
         if j < 2:
-            eb[j] = jnp.exp(-lb[j])
-            numbers = along + (blk, other)[j] * rows
+            source, owner, begin = j, (blk, other)[j], part * half
         else:
-            part = slice(0, half) if j == 2 else slice(half, rows)
-            eb[j] = jnp.exp(-jnp.concatenate([lb[2][:, part], lb[3][:, part]], axis=1))
-            begin = (j - 2) * half
-            numbers = jnp.where(along < half, along + (far * rows + begin), along + (far_other * rows + begin - half))
-        ids[j] = numbers.astype(F32)
+            source, owner, begin = 2 + part, (far, far_other)[part], (j - 2) * half
+        eb[j, :, part * half : part * half + half] = jnp.exp(-lb[source, :, begin : begin + half])
+        along = lax.broadcasted_iota(jnp.int32, (1, half), 1)
+        ids[j, :, part * half : part * half + half] = (along + (owner * rows + begin)).astype(F32)
 
     begun = set()
 
@@ -97,41 +95,45 @@
             into[...] = term
         begun.add(key)
 
-    def raw_scores(group, j):
-        return lax.dot_general(ua[group], ub[j], NT, preferred_element_type=F32)
-
-    def spend(raw, group, j):
+    def raw_scores(group, j, part):
+        return lax.dot_general(ua[group], ub[j, pl.ds(part * half, half)], NT, preferred_element_type=F32)
+
+    def spend(raw, group, j, part):
+        here = pl.ds(part * half, half)
+        along = slice(part * half, part * half + half)
         chance = jnp.exp2(raw * scale)
-        reps = rows // 128
-        weight = jnp.concatenate([ea_col[group]] * reps, axis=1) + eb[j]
-        paired = jnp.concatenate([match_col[group]] * reps, axis=1) == ids[j]
+        reps = half // 128
+        weight = jnp.concatenate([ea_col[group]] * reps, axis=1) + eb[j, :, along]
+        paired = jnp.concatenate([match_col[group]] * reps, axis=1) == ids[j, :, along]
         value = chance * weight
         coupling = jnp.where(paired, value - 2.0, value).astype(BF)
-        rows_term = jnp.dot(coupling, ub[j], preferred_element_type=F32)
+        rows_term = jnp.dot(coupling, ub[j, here], preferred_element_type=F32)
         add(da_own if group == 0 else da.at[group - 1], rows_term, ("a", group))
         columns_term = lax.dot_general(coupling, ua[group], TN, preferred_element_type=F32)
-        add(db_own if j == 0 else db.at[j - 1], columns_term, ("b", j))
+        add((db_own if j == 0 else db.at[j - 1]).at[here], columns_term, ("b", j, part))
 
     def pairs(*todo):
-        ahead = raw_scores(*todo[0])
-        for k, (group, j) in enumerate(todo):
+        units = []
+        for group, j, *part in todo:
+            units += [(group, j, p) for p in (part or (0, 1))]
+        ahead = raw_scores(*units[0])
+        for k, unit in enumerate(units):
             raw = ahead
-            if k + 1 < len(todo):
-                ahead = raw_scores(*todo[k + 1])
-            spend(raw, group, j)
+            if k + 1 < len(units):
+                ahead = raw_scores(*units[k + 1])
+            spend(raw, *unit)
 
     pl.semaphore_wait(barrier, 4)
     quarters = [pl.ds(k * quarter, quarter) for k in range(4)]
+    small_left = [send(match_hbm, match.at[2], left), send(la_hbm, la.at[2], left)]
+    small_right = [send(match_hbm, match.at[1], right), send(la_hbm, la.at[1], right)]
+    lb_other = send(lb_hbm, lb.at[1], other)
+    lb_far = send(lb_hbm, lb.at[2], far)
     early_right = [send(a_hbm.at[quarters[k]], a_in.at[0, quarters[k]], right) for k in (0, 1)]
     early_left = [send(a_hbm.at[quarters[k]], a_in.at[0, quarters[k]], left) for k in (2, 3)]
     b_other = send(b_hbm, b_in.at[0], other)
     far_a = send(b_hbm.at[first], b_in.at[1, first], far)
-    small_left = [send(match_hbm, match.at[2], left), send(la_hbm, la.at[2], left)]
-    small_right = [send(match_hbm, match.at[1], right), send(la_hbm, la.at[1], right)]
-    lb_other = send(lb_hbm, lb.at[1], other)
-    lb_far = send(lb_hbm, lb.at[2], far)
-    late_left = send(a_hbm.at[first], a_in.at[2, second], left)
-    late_right = send(a_hbm.at[second], a_in.at[2, first], right)
+    far_b = send(b_hbm.at[second], b_in.at[2, first], far)
 
     for load in loads:
         load.wait()
@@ -141,7 +143,8 @@
     scale = math.log2(math.e) / jnp.broadcast_to(temperature, (1, 1))
     scale_out[...] = jnp.broadcast_to(1.0 / jnp.broadcast_to(temperature, (1, 1)), (8, 128))
     take_a(0, [(0, 0), (0, 1), (0, 2), (0, 3)])
-    take_b(0)
+    take_b(0, 0)
+    take_b(0, 1)
     pairs((0, 0))
 
     opp = []
@@ -150,7 +153,6 @@
         opp.append(send(a_in.at[0, quarters[k]], a_in.at[1, quarters[k]], right))
         early_left[k].wait_recv()
         opp.append(send(a_in.at[0, quarters[k + 2]], a_in.at[1, quarters[k + 2]], left))
-    far_b = send(b_hbm.at[second], b_in.at[2, first], far)
     for copy in small_left + small_right:
         copy.wait_recv()
     small_on = [send(match.at[1], match.at[3], right), send(la.at[1], la.at[3], right)]
@@ -159,42 +161,48 @@
     b_other.wait_recv()
     lb_other.wait_recv()
 
-    take_b(1)
+    take_b(1, 0)
+    take_b(1, 1)
     take_a(1, [(1, 0), (1, 1), (2, 2), (2, 3)])
-    pairs((0, 1), (1, 0), (1, 1))
-
+    pairs((0, 1), (1, 0))
+
+    late_left = send(a_hbm.at[first], a_in.at[2, second], left)
+    late_right = send(a_hbm.at[second], a_in.at[2, first], right)
     far_a.wait_recv()
     far_a_on = send(b_in.at[1, first], b_in.at[1, second], other)
-    lb_on.wait_recv()
-    far_a_on.wait_recv()
-    take_b(2)
-    pairs((0, 2), (1, 2))
+    take_b(2, 0)
+    pairs((1, 1), (1, 2, 0), (0, 2, 0))
 
     far_b.wait_recv()
     far_b_on = send(b_in.at[2, first], b_in.at[2, second], other)
     for copy in small_on + opp:
         copy.wait_recv()
+    lb_on.wait_recv()
+    far_a_on.wait_recv()
     take_a(2, [(3, 0), (3, 1), (3, 2), (3, 3)])
-    pairs((2, 0), (2, 1))
+    take_b(2, 1)
+    take_b(3, 0)
+    pairs((2, 0), (2, 1), (2, 2), (2, 3, 0))
 
     far_b_on.wait_recv()
-    take_b(3)
-    pairs((2, 2), (2, 3))
+    take_b(3, 1)
+    pairs((2, 3, 1))
     da_out[1] = da[1].astype(BF)
     part_right = send(da_out.at[1, first], opp_in.at[first], right)
     part_left = send(da_out.at[1, second], opp_in.at[second], left)
+    pairs((1, 3, 0), (1, 3, 1), (1, 2, 1))
+    da_out[0] = da[0].astype(BF)
+    sum_left = send(da_out.at[0, first], da_right.at[first], left)
+    sum_right = send(da_out.at[0, second], da_left.at[second], right)
 
     late_left.wait_recv()
     late_right.wait_recv()
     take_a(3, [(1, 2), (1, 3), (2, 0), (2, 1)])
-    pairs((3, 2), (1, 3))
+    pairs((0, 2, 1), (3, 2, 1), (3, 2, 0))
     db_out[0] = db[1, half:rows].astype(BF)
     core_a = send(db_out.at[0], core_in.at[0], other)
-    da_out[0] = da[0].astype(BF)
-    sum_left = send(da_out.at[0, first], da_right.at[first], left)
-    sum_right = send(da_out.at[0, second], da_left.at[second], right)
-
-    pairs((0, 3), (3, 3))
+
+    pairs((0, 3, 1), (3, 3, 1), (0, 3, 0), (3, 3, 0))
     db_out[1] = db[2, half:rows].astype(BF)
     core_b = send(db_out.at[1], core_in.at[1], other)
     core_a.wait_recv()

time: 33.4 us -> 31.6 us (0.946)
  Pallas kernels: 32 us -> 30.2 us
    pallas_call x1, Pallas kernels: 30.6 us -> 28.9 us  [on_device(): pl.pallas_call(exchange_kernel, out_shape=(jax.ShapeDtypeStruct((8, 128),...]
where the time goes in v3:
time: 31.6 us; the launch traced here: 31.5 us
  Pallas kernels  30.2 us (96%)
  between operations  1.29 us (4%)
    pallas_call x1, Pallas kernels, on_device(): pl.pallas_call(exchange_kernel, out_shape=(jax.ShapeDtypeStruct((8, 128),...  28.9 us
    pallas_call x1, Pallas kernels, on_device(): pl.pallas_call(finish_kernel, out_shape=(jax.ShapeDtypeStruct((rows, widt...  1.33 us

profile of v3, /device:TPU:1, one launch (start us, length us, event | category | flops | bytes accessed | tf_op | source)
XLA Modules:
  0.0 31.5 jit_solution(12022627021202118340)
XLA Ops:
  1.3 28.9 %shard_map.86 = (f32[8,128]{1,0:T(8,128)S(1)}, bf16[512,256]{1,0:T(8,128)(2,1)S(1)}, bf16[512,256]{1,0:T(8,128)(2,1)S(1)}, f32[512,256]{1,0:T(8,128)S(1)}, bf16[...) custom-call(bf16[512,256]{1,0:T(8,128)(2,1)} %a_hbm.1, ...), custom_call_target="tpu_custom_call" | custom-call | tf_op jit(solution)/shard_map/pallas_call | solution.py:264
  30.1 1.3 %shard_map.87 = (f32[512,256]{1,0:T(8,128)}, f32[512,256]{1,0:T(8,128)}) custom-call(f32[8,128]{1,0:T(8,128)S(1)} %get-tuple-element.11.scale, bf16[512,256]{1,0:T(8,128)(2,1)S(1)} %get-tuple-element.12.a, bf16[512,256]{1,0:T(8,128)(2,1)S(1)} %get-tuple-element.13.b, f32[512,256]{1,0:T(8,128)S(1)} %get-tuple-element.14.da_own, ...), custom_call_target="tpu_custom_call" | custom-call | tf_op jit(solution)/shard_map/pallas_call | solution.py:318

commit v4 on v3

--- a/solution.py
+++ b/solution.py
@@ -175,13 +175,15 @@
 
     far_b.wait_recv()
     far_b_on = send(b_in.at[2, first], b_in.at[2, second], other)
+    lb_on.wait_recv()
+    far_a_on.wait_recv()
+    take_b(2, 1)
+    take_b(3, 0)
+    pairs((1, 2, 1), (0, 2, 1))
+
     for copy in small_on + opp:
         copy.wait_recv()
-    lb_on.wait_recv()
-    far_a_on.wait_recv()
     take_a(2, [(3, 0), (3, 1), (3, 2), (3, 3)])
-    take_b(2, 1)
-    take_b(3, 0)
     pairs((2, 0), (2, 1), (2, 2), (2, 3, 0))
 
     far_b_on.wait_recv()
@@ -190,24 +192,24 @@
     da_out[1] = da[1].astype(BF)
     part_right = send(da_out.at[1, first], opp_in.at[first], right)
     part_left = send(da_out.at[1, second], opp_in.at[second], left)
-    pairs((1, 3, 0), (1, 3, 1), (1, 2, 1))
+    late_left.wait_recv()
+    late_right.wait_recv()
+    take_a(3, [(1, 2), (1, 3), (2, 0), (2, 1)])
+    pairs((3, 2, 1), (3, 2, 0))
+    db_out[0] = db[1, half:rows].astype(BF)
+    core_a = send(db_out.at[0], core_in.at[0], other)
+
+    pairs((1, 3), (0, 3))
     da_out[0] = da[0].astype(BF)
     sum_left = send(da_out.at[0, first], da_right.at[first], left)
     sum_right = send(da_out.at[0, second], da_left.at[second], right)
-
-    late_left.wait_recv()
-    late_right.wait_recv()
-    take_a(3, [(1, 2), (1, 3), (2, 0), (2, 1)])
-    pairs((0, 2, 1), (3, 2, 1), (3, 2, 0))
-    db_out[0] = db[1, half:rows].astype(BF)
-    core_a = send(db_out.at[0], core_in.at[0], other)
-
-    pairs((0, 3, 1), (3, 3, 1), (0, 3, 0), (3, 3, 0))
-    db_out[1] = db[2, half:rows].astype(BF)
-    core_b = send(db_out.at[1], core_in.at[1], other)
     core_a.wait_recv()
     db_out[2] = (db[1, 0:half] + core_in[0].astype(F32)).astype(BF)
     sum_far_a = send(db_out.at[2], db_far.at[first], far)
+
+    pairs((3, 3, 1), (3, 3, 0))
+    db_out[1] = db[2, half:rows].astype(BF)
+    core_b = send(db_out.at[1], core_in.at[1], other)
 
     pairs((3, 1), (3, 0))
     core_b.wait_recv()

time: 31.6 us -> 31 us (0.981)
  Pallas kernels: 30.2 us -> 29.6 us
    pallas_call x1, Pallas kernels: 28.9 us -> 28.3 us  [on_device(): pl.pallas_call(exchange_kernel, out_shape=(jax.ShapeDtypeStruct((8, 128),...]
where the time goes in v4:
time: 31 us; the launch traced here: 30.9 us
  Pallas kernels  29.6 us (95%)
  between operations  1.29 us (4%)
    pallas_call x1, Pallas kernels, on_device(): pl.pallas_call(exchange_kernel, out_shape=(jax.ShapeDtypeStruct((8, 128),...  28.3 us
    pallas_call x1, Pallas kernels, on_device(): pl.pallas_call(finish_kernel, out_shape=(jax.ShapeDtypeStruct((rows, widt...  1.33 us

profile of v4, /device:TPU:1, one launch (start us, length us, event | category | flops | bytes accessed | tf_op | source)
XLA Modules:
  0.0 30.9 jit_solution(10626941506383561548)
XLA Ops:
  1.3 28.3 %shard_map.86 = (f32[8,128]{1,0:T(8,128)S(1)}, bf16[512,256]{1,0:T(8,128)(2,1)S(1)}, bf16[512,256]{1,0:T(8,128)(2,1)S(1)}, f32[512,256]{1,0:T(8,128)S(1)}, bf16[...) custom-call(bf16[512,256]{1,0:T(8,128)(2,1)} %a_hbm.1, ...), custom_call_target="tpu_custom_call" | custom-call | tf_op jit(solution)/shard_map/pallas_call | solution.py:266
  29.6 1.3 %shard_map.87 = (f32[512,256]{1,0:T(8,128)}, f32[512,256]{1,0:T(8,128)}) custom-call(f32[8,128]{1,0:T(8,128)S(1)} %get-tuple-element.11.scale, bf16[512,256]{1,0:T(8,128)(2,1)S(1)} %get-tuple-element.12.a, bf16[512,256]{1,0:T(8,128)(2,1)S(1)} %get-tuple-element.13.b, f32[512,256]{1,0:T(8,128)S(1)} %get-tuple-element.14.da_own, ...), custom_call_target="tpu_custom_call" | custom-call | tf_op jit(solution)/shard_map/pallas_call | solution.py:320

commit v5 on v4

--- a/solution.py
+++ b/solution.py
@@ -146,6 +146,11 @@
     take_b(0, 0)
     take_b(0, 1)
     pairs((0, 0))
+    b_other.wait_recv()
+    lb_other.wait_recv()
+    take_b(1, 0)
+    take_b(1, 1)
+    pairs((0, 1))
 
     opp = []
     for k in (0, 1):
@@ -158,20 +163,16 @@
     small_on = [send(match.at[1], match.at[3], right), send(la.at[1], la.at[3], right)]
     lb_far.wait_recv()
     lb_on = send(lb.at[2], lb.at[3], other)
-    b_other.wait_recv()
-    lb_other.wait_recv()
-
-    take_b(1, 0)
-    take_b(1, 1)
+
     take_a(1, [(1, 0), (1, 1), (2, 2), (2, 3)])
-    pairs((0, 1), (1, 0))
+    pairs((1, 0), (1, 1))
 
     late_left = send(a_hbm.at[first], a_in.at[2, second], left)
     late_right = send(a_hbm.at[second], a_in.at[2, first], right)
     far_a.wait_recv()
     far_a_on = send(b_in.at[1, first], b_in.at[1, second], other)
     take_b(2, 0)
-    pairs((1, 1), (1, 2, 0), (0, 2, 0))
+    pairs((1, 2, 0), (0, 2, 0))
 
     far_b.wait_recv()
     far_b_on = send(b_in.at[2, first], b_in.at[2, second], other)

time: 31 us -> 30.6 us (0.987)
  Pallas kernels: 29.6 us -> 29.2 us
    pallas_call x1, Pallas kernels: 28.3 us -> 27.9 us  [on_device(): pl.pallas_call(exchange_kernel, out_shape=(jax.ShapeDtypeStruct((8, 128),...]
where the time goes in v5:
time: 30.6 us; the launch traced here: 30.5 us
  Pallas kernels  29.2 us (95%)
  between operations  1.29 us (4%)
    pallas_call x1, Pallas kernels, on_device(): pl.pallas_call(exchange_kernel, out_shape=(jax.ShapeDtypeStruct((8, 128),...  27.9 us
    pallas_call x1, Pallas kernels, on_device(): pl.pallas_call(finish_kernel, out_shape=(jax.ShapeDtypeStruct((rows, widt...  1.33 us

profile of v5, /device:TPU:1, one launch (start us, length us, event | category | flops | bytes accessed | tf_op | source)
XLA Modules:
  0.0 30.5 jit_solution(11224853011997563768)
XLA Ops:
  1.3 27.9 %shard_map.86 = (f32[8,128]{1,0:T(8,128)S(1)}, bf16[512,256]{1,0:T(8,128)(2,1)S(1)}, bf16[512,256]{1,0:T(8,128)(2,1)S(1)}, f32[512,256]{1,0:T(8,128)S(1)}, bf16[...) custom-call(bf16[512,256]{1,0:T(8,128)(2,1)} %a_hbm.1, ...), custom_call_target="tpu_custom_call" | custom-call | tf_op jit(solution)/shard_map/pallas_call | solution.py:267
  29.2 1.3 %shard_map.87 = (f32[512,256]{1,0:T(8,128)}, f32[512,256]{1,0:T(8,128)}) custom-call(f32[8,128]{1,0:T(8,128)S(1)} %get-tuple-element.11.scale, bf16[512,256]{1,0:T(8,128)(2,1)S(1)} %get-tuple-element.12.a, bf16[512,256]{1,0:T(8,128)(2,1)S(1)} %get-tuple-element.13.b, f32[512,256]{1,0:T(8,128)S(1)} %get-tuple-element.14.da_own, ...), custom_call_target="tpu_custom_call" | custom-call | tf_op jit(solution)/shard_map/pallas_call | solution.py:321

commit v6 on v5

--- a/solution.py
+++ b/solution.py
@@ -236,7 +236,7 @@
     scale, a, b, da_own, da_left, da_right, db_own, db_core, db_far, out_a, out_b, result, sems
 ):
     rows = a.shape[0]
-    half = rows // 2
+    quarter = rows // 4
     by_temperature = scale[0:1, 0:1]
 
     def tangent(block, total):
@@ -248,11 +248,11 @@
     for which, (block, total, parts, out) in enumerate(
         ((b, db_own, (db_core, db_far), out_b), (a, da_own, (da_left, da_right), out_a))
     ):
-        for k in range(2):
-            part = pl.ds(k * half, half)
+        for k in range(4):
+            part = pl.ds(k * quarter, quarter)
             summed = total[part] + parts[0][part].astype(F32) + parts[1][part].astype(F32)
             result[which, part] = tangent(block[part], summed)
-            copies.append(pltpu.make_async_copy(result.at[which, part], out.at[part], sems.at[2 * which + k]))
+            copies.append(pltpu.make_async_copy(result.at[which, part], out.at[part], sems.at[4 * which + k]))
             copies[-1].start()
     for copy in copies:
         copy.wait()
@@ -323,7 +323,7 @@
         out_shape=(jax.ShapeDtypeStruct((rows, width), F32), jax.ShapeDtypeStruct((rows, width), F32)),
         in_specs=[vmem] * 9,
         out_specs=[anywhere] * 2,
-        scratch_shapes=[pltpu.VMEM((2, rows, width), F32), dma((4,))],
+        scratch_shapes=[pltpu.VMEM((2, rows, width), F32), dma((8,))],
         compiler_params=pltpu.CompilerParams(vmem_limit_bytes=32 << 20),
     )(*pieces)
 

time: 30.6 us -> 30.7 us (level)
  no operation moved by 1% of the time
where the time goes in v6:
time: 30.7 us; the launch traced here: 30.6 us
  Pallas kernels  29.3 us (95%)
  between operations  1.29 us (4%)
    pallas_call x1, Pallas kernels, on_device(): pl.pallas_call(exchange_kernel, out_shape=(jax.ShapeDtypeStruct((8, 128),...  27.9 us
    pallas_call x1, Pallas kernels, on_device(): pl.pallas_call(finish_kernel, out_shape=(jax.ShapeDtypeStruct((rows, widt...  1.38 us

profile of v6, /device:TPU:1, one launch (start us, length us, event | category | flops | bytes accessed | tf_op | source)
XLA Modules:
  0.0 30.6 jit_solution(10079917594089717709)
XLA Ops:
  1.3 27.9 %shard_map.86 = (f32[8,128]{1,0:T(8,128)S(1)}, bf16[512,256]{1,0:T(8,128)(2,1)S(1)}, bf16[512,256]{1,0:T(8,128)(2,1)S(1)}, f32[512,256]{1,0:T(8,128)S(1)}, bf16[...) custom-call(bf16[512,256]{1,0:T(8,128)(2,1)} %a_hbm.1, ...), custom_call_target="tpu_custom_call" | custom-call | tf_op jit(solution)/shard_map/pallas_call | solution.py:267
  29.2 1.4 %shard_map.87 = (f32[512,256]{1,0:T(8,128)}, f32[512,256]{1,0:T(8,128)}) custom-call(f32[8,128]{1,0:T(8,128)S(1)} %get-tuple-element.11.scale, bf16[512,256]{1,0:T(8,128)(2,1)S(1)} %get-tuple-element.12.a, bf16[512,256]{1,0:T(8,128)(2,1)S(1)} %get-tuple-element.13.b, f32[512,256]{1,0:T(8,128)S(1)} %get-tuple-element.14.da_own, ...), custom_call_target="tpu_custom_call" | custom-call | tf_op jit(solution)/shard_map/pallas_call | solution.py:321
